TPU v7x, 32 devices: a whole 2x2x4 slice. The times are simulated.
32 devices in a mesh: chan: 16 (over z, x, core), img: 2 (over y).
Axes of the slice: x: 2, y: 2, z: 4, core: 2. Of those that a mesh axis runs over, the one named last changes fastest.
Arguments:
- tokens: bfloat16 [32, 512, 1024], P('chan', 'img'), may hold values from -6 to 6
- chan_embed: float32 [32, 1024], P('chan'), may hold values from -6 to 6
- value_proj: bfloat16 [1024, 1024], replicated, may hold values from -0.1875 to 0.1875
- key_query: bfloat16 [1024, 16], replicated, may hold values from -0.1875 to 0.1875
- chan_bias: float32 [32, 16], replicated, may hold values from -5 to 400
- cotangent: bfloat16 [512, 1024], P(('img', 'chan')), may hold values from -96 to 96
Outputs:
- grad_input: bfloat16 [32, 512, 1024], P('chan', 'img')
- grad_embed: float32 [32, 1024], P('chan')
- grad_bias: float32 [32, 16], P('chan')
All inputs are finite; a program needn't handle non-finite values.
Results may differ from a plain program's by a relative error of at most 0.007.
Values may be sent and summed in bfloat16 or wider, within the bound.
A program may use at most 64 MiB of HBM per device.

v0:
```python
import jax
import jax.numpy as jnp
from jax import lax
from jax.sharding import PartitionSpec as P


def merged(value, axis, join):
    pieces = jax.tree.map(lambda part: lax.all_gather(part, axis), value)
    head = jax.tree.map(lambda part: part[0], pieces)
    tail = jax.tree.map(lambda part: part[1:], pieces)
    running, _ = lax.scan(lambda running, slab: (join(running, slab), None), head, tail)
    return running


def head_parts(shifted, grad_rows, value_proj, key_query, local_bias):
    num_chans, num_rows, model_width = shifted.shape
    num_heads = key_query.shape[1]
    flat_rows = shifted.reshape(num_chans * num_rows, model_width)
    values = jnp.dot(flat_rows, value_proj, preferred_element_type=jnp.float32).astype(jnp.bfloat16)
    values = values.reshape(num_chans, num_rows, num_heads, model_width // num_heads)
    scores = jnp.dot(flat_rows, key_query, preferred_element_type=jnp.float32).reshape(
        num_chans, num_rows, num_heads
    )
    scores = scores + local_bias[:, None, :]
    grad_heads = grad_rows.reshape(num_rows, num_heads, model_width // num_heads)
    prob_grad = jnp.einsum("cthk,thk->cth", values, grad_heads, preferred_element_type=jnp.float32)
    return (scores, prob_grad, grad_heads)


def input_grads(soft_weights, score_grad, grad_heads, value_proj, key_query):
    num_chans, num_rows, num_heads = soft_weights.shape
    model_width = value_proj.shape[0]
    value_grad = (soft_weights[..., None] * grad_heads.astype(jnp.float32)[None]).astype(
        jnp.bfloat16
    )
    value_grad = value_grad.reshape(num_chans * num_rows, model_width)
    score_grad_b = score_grad.astype(jnp.bfloat16).reshape(num_chans * num_rows, num_heads)
    contract = (((1,), (1,)), ((), ()))
    grad_sum = lax.dot_general(value_grad, value_proj, contract, preferred_element_type=jnp.float32)
    grad_sum = grad_sum + lax.dot_general(
        score_grad_b, key_query, contract, preferred_element_type=jnp.float32
    )
    return grad_sum.astype(jnp.bfloat16).reshape(num_chans, num_rows, model_width)


def combine_totals(first, second):
    peak_both = jnp.maximum(first[0], second[0])
    scale_first = jnp.exp(first[0] - peak_both)
    scale_second = jnp.exp(second[0] - peak_both)
    return (
        peak_both,
        first[1] * scale_first + second[1] * scale_second,
        first[2] * scale_first + second[2] * scale_second,
    )


def body(tokens, chan_embed, value_proj, key_query, chan_bias, cotangent):
    num_chans = tokens.shape[0]
    shifted = (tokens.astype(jnp.float32) + chan_embed[:, None, :]).astype(jnp.bfloat16)
    full_cotangent = lax.all_gather(cotangent, "chan", axis=0, tiled=True)
    first_row = lax.axis_index("chan") * num_chans
    local_bias = lax.dynamic_slice_in_dim(chan_bias, first_row, num_chans, 0)
    scores, prob_grad, grad_heads = head_parts(
        shifted, full_cotangent, value_proj, key_query, local_bias
    )
    peak_local = jnp.max(scores, axis=0)
    exp_local = jnp.exp(scores - peak_local[None])
    peak_score, exp_total, weighted_grad = merged(
        (peak_local, jnp.sum(exp_local, axis=0), jnp.sum(exp_local * prob_grad, axis=0)),
        "chan",
        combine_totals,
    )
    soft_weights = jnp.exp(scores - peak_score[None]) / exp_total[None]
    score_grad = soft_weights * (prob_grad - (weighted_grad / exp_total)[None])
    grad_input = input_grads(soft_weights, score_grad, grad_heads, value_proj, key_query)
    bias_part = jnp.sum(score_grad, axis=1)
    embed_part = jnp.sum(grad_input.astype(jnp.float32), axis=1)
    grad_embed, grad_bias = lax.psum((embed_part, bias_part), "img")
    return (grad_input, grad_embed, grad_bias)


def solution(mesh):
    in_specs = (P("chan", "img", None), P("chan", None), P(), P(), P(), P(("img", "chan"), None))
    out_specs = (P("chan", "img", None), P("chan", None), P("chan", None))
    return jax.shard_map(body, mesh=mesh, in_specs=in_specs, out_specs=out_specs, check_vma=False)
```

profile of v0, /device:TPU:0, one launch (start us, length us, event | category | flops | bytes accessed | tf_op | source)
XLA Modules:
  0.0 140.1 jit_solution(6937604624711978473)
XLA Ops:
  1.7 1.5 %add_convert_fusion.1 = bf16[2,256,1024]{2,1,0:T(8,128)(2,1)S(1)} fusion(bf16[2,256,1024]{2,1,0:T(8,128)(2,1)} %param.8, f32[2,1024]{1,0:T(2,128)} %param.9), kind=kLoop, calls=%fused_computation.17 | loop fusion | flops 1572864 | bytes 2105344 | tf_op jit(solution)/shard_map/convert_element_type | solution.py:59
  3.5 2.3 %convolution_convert_fusion = bf16[512,1024]{1,0:T(8,128)(2,1)} fusion(bf16[512,1024]{1,0:T(8,128)(2,1)S(1)} %bitcast.76, bf16[1024,1024]{1,0:T(8,128)(2,1)S(1)} %copy-done), kind=kOutput, calls=%fused_computation.18 | convolution fusion | flops 1074266112 | bytes 4194304 | tf_op jit(solution)/shard_map/dot_general | solution.py:19
  5.8 1.5 %copy.20 = bf16[512,1024]{0,1:T(8,128)(2,1)S(1)} copy(bf16[512,1024]{1,0:T(8,128)(2,1)} %convolution_convert_fusion) | data formatting | bytes 2097152 | tf_op jit(solution)/shard_map/convert_element_type | solution.py:19
  7.3 1.1 reshape.42
  8.4 24.6 %all_gather.25 = bf16[256,1024]{1,0:T(8,128)(2,1)S(1)} all-gather(bf16[16,1024]{1,0:T(8,128)(2,1)S(1)} %copy-done.6), channel_id=1, replica_groups=mesh['chan'=16,'img'=2] {'chan'}, dimensions={0}, use_global_device_ids=true | all-gather | bytes 557056 | tf_op jit(solution)/shard_map/all_gather | solution.py:60
  33.0 1.0 copy.21
  34.0 1.2 bitcast_convert_fusion
  35.3 1.2 multiply_reduce_fusion
  36.5 18.2 %all-gather.1 = f32[4096,16]{0,1:T(8,128)S(1)} all-gather(f32[256,16]{0,1:T(8,128)S(1)} %get-tuple-element.60), channel_id=3, replica_groups=mesh['chan'=16,'img'=2] {'chan'}, dimensions={0}, use_global_device_ids=true | all-gather | bytes 278528 | tf_op jit(solution)/shard_map/all_gather | solution.py:8
  55.4 1.7 %reshape.56 = f32[15,256,16]{1,0,2:T(8,128)} reshape(f32[3840,16]{0,1:T(8,128)} %slice.34) | data formatting | bytes 491520 | tf_op jit(solution)/shard_map/slice | solution.py:10
  57.1 19.5 %all-gather.2 = f32[4096,16]{0,1:T(8,128)S(1)} all-gather(f32[256,16]{0,1:T(8,128)S(1)} %get-tuple-element.59), channel_id=4, replica_groups=mesh['chan'=16,'img'=2] {'chan'}, dimensions={0}, use_global_device_ids=true | all-gather | bytes 278528 | tf_op jit(solution)/shard_map/all_gather | solution.py:8
  78.0 1.7 %reshape.57 = f32[15,256,16]{1,0,2:T(8,128)} reshape(f32[3840,16]{0,1:T(8,128)} %slice.35) | data formatting | bytes 491520 | tf_op jit(solution)/shard_map/slice | solution.py:10
  80.4 18.1 %all-gather = f32[4096,16]{0,1:T(8,128)S(1)} all-gather(f32[256,16]{0,1:T(8,128)S(1)} %get-tuple-element.83), channel_id=2, replica_groups=mesh['chan'=16,'img'=2] {'chan'}, dimensions={0}, use_global_device_ids=true | all-gather | bytes 278528 | tf_op jit(solution)/shard_map/all_gather | solution.py:8
  99.3 1.7 %reshape.55 = f32[15,256,16]{1,0,2:T(8,128)} reshape(f32[3840,16]{0,1:T(8,128)} %slice.33) | data formatting | bytes 491520 | tf_op jit(solution)/shard_map/slice | solution.py:10
  101.0 30.0 %while.14 = (s32[]{:T(128)}, f32[256,16]{0,1:T(8,128)S(1)}, f32[256,16]{0,1:T(8,128)S(1)}, f32[256,16]{0,1:T(8,128)S(1)}, f32[15,256,16]{1,0,2:T(8,128)}, /*inde...) while((s32[]{:T(128)}, f32[256,16]{0,1:T(8,128)S(1)}, f32[256,16]{0,1:T(8,128)S(1)}, ...), condition=%wide.region_4.5_spmd, body=%wide.region_3.4_spmd.sunk | while | flops 45058 | bytes 327773 | solution.py:11
  101.0 1.0 constant_dynamic-slice_fusion.6
  103.0 1.0 constant_dynamic-slice_fusion.6
  105.0 1.0 constant_dynamic-slice_fusion.6
  107.0 1.0 constant_dynamic-slice_fusion.6
  109.1 1.0 constant_dynamic-slice_fusion.6
  111.1 1.0 constant_dynamic-slice_fusion.6
  113.1 1.0 constant_dynamic-slice_fusion.6
  115.1 1.0 constant_dynamic-slice_fusion.6
  117.1 1.0 constant_dynamic-slice_fusion.6
  119.1 1.0 constant_dynamic-slice_fusion.6
  121.1 1.0 constant_dynamic-slice_fusion.6
  123.1 1.0 constant_dynamic-slice_fusion.6
  125.1 1.0 constant_dynamic-slice_fusion.6
  127.1 1.0 constant_dynamic-slice_fusion.6
  129.1 1.0 constant_dynamic-slice_fusion.6
  132.5 1.3 fusion.12
  134.5 5.7 %all-reduce = (f32[2,1024]{1,0:T(2,128)}, f32[2,16]{1,0:T(2,128)}) all-reduce(f32[2,1024]{1,0:T(2,128)S(1)} %convert_reduce_fusion, f32[2,16]{1,0:T(2,128)S(1)} %get-tuple-element.79), channel_id=1, replica_groups=mesh['chan'=16,'img'=2] {'img'}, use_global_device_ids=true, to_apply=%region_6.7 | all-reduce | flops 2080 | bytes 16640 | tf_op jit(solution)/shard_map/psum | solution.py:78
  (93 shorter events, 21.6 us)
Async XLA Ops:
  0.6 2.9 %copy-start = (bf16[1024,1024]{1,0:T(8,128)(2,1)S(1)}, bf16[1024,1024]{1,0:T(8,128)(2,1)}, u32[]{:S(2)}) copy-start(bf16[1024,1024]{1,0:T(8,128)(2,1)} %param.10) | copy-start | bytes 6291460
  0.6 2.5 %copy-start.4 = (bf16[1024,16]{0,1:T(8,128)(2,1)S(1)}, bf16[1024,16]{0,1:T(8,128)(2,1)}, u32[]{:S(2)}) copy-start(bf16[1024,16]{0,1:T(8,128)(2,1)} %param.11) | copy-start | bytes 98308
  5.8 2.6 %copy-start.6 = (bf16[16,1024]{1,0:T(8,128)(2,1)S(1)}, bf16[16,1024]{1,0:T(8,128)(2,1)}, u32[]{:S(2)}) copy-start(bf16[16,1024]{1,0:T(8,128)(2,1)} %param.13) | copy-start | bytes 98308
  33.9 1.4 copy-start.2
  76.6 0.7 copy-start.3
  132.5 1.3 copy-start.5
  134.2 5.9 %copy-start.1 = (bf16[512,1024]{1,0:T(8,128)(2,1)}, bf16[512,1024]{1,0:T(8,128)(2,1)S(1)}, u32[]{:S(2)}) copy-start(bf16[512,1024]{1,0:T(8,128)(2,1)S(1)} %add_convert_fusion) | copy-start | bytes 3145732
where the time goes:
time: 141 us; the launch traced here: 140 us
  blocking collectives  86 us (61%)
  local copies, waits for them, and re-layouts  42.7 us (30%)
  other arithmetic  5.67 us (4%)
  matrix products  4.38 us (3%)
    all_gather x3, blocking collectives, merged(): pieces = jax.tree.map(lambda part: lax.all_gather(part, axis), value)  55.8 us
    dynamic_slice x30, local copies, waits for them, and re-layouts, merged(): lax.scan(lambda running, slab: (join(running, slab), None), head, tail)  28.8 us
    all_gather x1, blocking collectives, body(): full_cotangent = lax.all_gather(cotangent, 'chan', axis=0, tiled=True)  24.6 us
    slice x6, local copies, waits for them, and re-layouts, merged(): tail = jax.tree.map(lambda part: part[1:], pieces)  7.35 us
    psum x1, blocking collectives, body(): grad_embed, grad_bias = lax.psum((embed_part, bias_part), 'img')  5.65 us

commit v1 on v0

v1 whole, which is shorter than its diff:
```python
import functools

import jax
import jax.numpy as jnp
from jax import lax
from jax.experimental import pallas as pl
from jax.experimental.pallas import tpu as pltpu
from jax.sharding import PartitionSpec as P

MESH = pl.DeviceIdType.MESH
F32 = jnp.float32
BF16 = jnp.bfloat16
ROWS_BY_ROWS = (((1,), (1,)), ((), ()))


def dot_t(left, right):
    return lax.dot_general(left, right, ROWS_BY_ROWS, preferred_element_type=F32)


def dot(left, right):
    return jnp.dot(left, right, preferred_element_type=F32)


def grid_of(n):
    chips = n // 2
    wide = 1
    while wide * wide * 4 <= chips:
        wide *= 2
    return chips // wide, wide


def kernel(
    n, g, gather,
    tokens, embed, proj, query, bias, cot,
    out_grad, out_embed, out_bias,
    tok, emb, pv, kq, bia, cots, shifted, values, vgrad, outv, oemb, obias,
    stat_out, stat_in, tot_out, tot_in, img_out, img_in,
    load_sem, store_sem, cot_send, cot_recv, stat_send, stat_recv, tot_send, tot_recv,
    img_send, img_recv,
):
    chans, toks, width = tokens.shape
    heads = query.shape[1]
    depth = width // heads
    tile = min(256, width)
    tiles = width // tile
    me = lax.axis_index("chan")
    my_img = lax.axis_index("img")
    rows = cot.shape[0]

    def load(slot, src, dst):
        copy = pltpu.make_async_copy(src, dst, load_sem.at[slot])
        copy.start()
        return copy

    if gather:
        cot_load = load(0, cot, cots.at[pl.ds(pl.multiple_of(me * rows, rows), rows)])
    else:
        cot_load = load(0, cot, cots)
    small_loads = [load(1, embed, emb), load(2, bias, bia), load(3, query, kq)]
    tok_loads = [load(4 + c, tokens.at[c], tok.at[pl.ds(c * toks, toks)]) for c in range(chans)]
    proj_loads = [
        load(
            4 + chans + j,
            proj.at[:, pl.ds(j * tile, tile)],
            pv.at[:, pl.ds(j * tile, tile)],
        )
        for j in range(tiles)
    ]

    barrier = pltpu.get_barrier_semaphore()
    for k in range(1, n):
        pl.semaphore_signal(
            barrier, inc=1, device_id={"chan": lax.rem(me + k, n)}, device_id_type=MESH
        )
    for k in range(1, g):
        pl.semaphore_signal(
            barrier, inc=1, device_id={"img": lax.rem(my_img + k, g)}, device_id_type=MESH
        )
    pl.semaphore_wait(barrier, n - 1 + g - 1)

    tall, wide = grid_of(n)
    core = lax.rem(me, 2)
    my_b = lax.rem(me // 2, wide)
    my_a = me // (2 * wide)

    def index(a, b, c):
        return (a * wide + b) * 2 + c

    sends = []

    def block(i):
        return cots.at[pl.ds(pl.multiple_of(i * rows, rows), rows)]

    def send(i, to, own=False):
        copy = pltpu.make_async_remote_copy(
            src_ref=cot if own else block(i),
            dst_ref=block(i),
            send_sem=cot_send.at[len(sends)],
            recv_sem=cot_recv.at[i],
            device_id={"chan": to},
            device_id_type=MESH,
        )
        copy.start()
        sends.append(copy)

    def arrive(i):
        pltpu.make_async_remote_copy(
            src_ref=cot,
            dst_ref=block(i),
            send_sem=cot_send.at[0],
            recv_sem=cot_recv.at[i],
            device_id={"chan": me},
            device_id_type=MESH,
        ).wait_recv()

    def others_a():
        return [lax.rem(my_a + k, tall) for k in range(1, tall)]

    def others_b():
        return [lax.rem(my_b + k, wide) for k in range(1, wide)]

    mate = index(my_a, my_b, 1 - core)
    if gather:
        for a in others_a():
            send(me, index(a, my_b, core), own=True)
        for b in others_b():
            send(me, index(my_a, b, core), own=True)
        send(me, mate, own=True)

    for copy in small_loads:
        copy.wait()
    kq_t = kq[...].astype(F32).T.astype(BF16)
    head_at = lax.broadcasted_iota(jnp.int32, (heads, width), 0) * depth
    lane_at = lax.broadcasted_iota(jnp.int32, (heads, width), 1)
    spread_f = jnp.where((lane_at >= head_at) & (lane_at < head_at + depth), 1.0, 0.0)
    spread = spread_f.astype(BF16)
    eye = lax.broadcasted_iota(jnp.int32, (heads, 128), 0) == lax.broadcasted_iota(
        jnp.int32, (heads, 128), 1
    )
    small_eye = lax.broadcasted_iota(jnp.int32, (heads, heads), 0) == lax.broadcasted_iota(
        jnp.int32, (heads, heads), 1
    )

    scores = []
    for c in range(chans):
        tok_loads[c].wait()
        at = pl.ds(c * toks, toks)
        moved = (tok[at, :].astype(F32) + emb[pl.ds(c, 1), :]).astype(BF16)
        shifted[at, :] = moved
        bias_row = bia[pl.ds(me * chans + c, 1), :]
        bias_col = jnp.sum(jnp.where(small_eye, bias_row, 0.0), axis=1, keepdims=True)
        scores.append(dot_t(kq_t, moved) + bias_col)

    def value_tile(j):
        proj_loads[j].wait()
        cols = pl.ds(j * tile, tile)
        values[:, cols] = dot(shifted[...], pv[:, cols]).astype(BF16)

    peak = functools.reduce(jnp.maximum, scores)
    exps = [jnp.exp(s - peak) for s in scores]
    exp_sum = functools.reduce(jnp.add, exps)

    done = 0
    if gather:
        steps = []
        for a in others_a():
            def forward(a=a):
                i = index(a, my_b, core)
                arrive(i)
                for b in others_b():
                    send(i, index(my_a, b, core))
                send(i, mate)
            steps.append(forward)
        for b in others_b():
            for k in range(tall):
                def pass_on(b=b, k=k):
                    i = index(lax.rem(my_a + k, tall), b, core)
                    arrive(i)
                    send(i, mate)
                steps.append(pass_on)
        value_tile(0)
        done = 1
        per_tile = -(-len(steps) // max(1, tiles - 1))
        at_step = 0
        while at_step < len(steps):
            for step in steps[at_step:at_step + per_tile]:
                step()
            at_step += per_tile
            if done < tiles:
                value_tile(done)
                done += 1
    while done < tiles:
        value_tile(done)
        done += 1
    cot_load.wait()
    if gather:
        for a in range(tall):
            for b in range(wide):
                arrive(index(a, b, 1 - core))

    cot_rows = cots[...]
    prob = []
    for c in range(chans):
        at = pl.ds(c * toks, toks)
        prob.append(dot_t(spread, values[at, :] * cot_rows))
    weighted = functools.reduce(jnp.add, [e * p for e, p in zip(exps, prob)])
    stat_out[:, 0, :] = peak
    stat_out[:, 1, :] = exp_sum
    stat_out[:, 2, :] = weighted

    stat_sends = []
    for k in range(1, n):
        to = lax.rem(me + k, n)
        copy = pltpu.make_async_remote_copy(
            src_ref=stat_out.at[lax.rem(to, heads)],
            dst_ref=stat_in.at[me],
            send_sem=stat_send.at[k],
            recv_sem=stat_recv.at[me],
            device_id={"chan": to},
            device_id_type=MESH,
        )
        stat_sends.append(copy)

        @pl.when(to < heads)
        def _(copy=copy):
            copy.start()

    def exchange_totals():
        stat_in[me] = stat_out[lax.rem(me, heads)]
        for k in range(1, n):
            frm = lax.rem(me + k, n)
            pltpu.make_async_remote_copy(
                src_ref=stat_out.at[0],
                dst_ref=stat_in.at[frm],
                send_sem=stat_send.at[0],
                recv_sem=stat_recv.at[frm],
                device_id={"chan": me},
                device_id_type=MESH,
            ).wait_recv()
        peaks = stat_in[:, 0, :]
        top = jnp.max(peaks, axis=0, keepdims=True)
        scale = jnp.exp(peaks - top)
        total = jnp.sum(stat_in[:, 1, :] * scale, axis=0, keepdims=True)
        mean = jnp.sum(stat_in[:, 2, :] * scale, axis=0, keepdims=True) / total
        tot_out[0:1, :] = top
        tot_out[1:2, :] = 1.0 / total
        tot_out[2:3, :] = mean
        copies = []
        for k in range(1, n):
            copy = pltpu.make_async_remote_copy(
                src_ref=tot_out,
                dst_ref=tot_in.at[lax.rem(me, heads)],
                send_sem=tot_send.at[k],
                recv_sem=tot_recv.at[lax.rem(me, heads)],
                device_id={"chan": lax.rem(me + k, n)},
                device_id_type=MESH,
            )
            copy.start()
            copies.append(copy)
        tot_in[lax.rem(me, heads)] = tot_out[...]
        for copy in copies:
            copy.wait_send()

    if n == heads:
        exchange_totals()
    else:
        pl.when(me < heads)(exchange_totals)

    def total_arrives(h):
        pltpu.make_async_remote_copy(
            src_ref=tot_out,
            dst_ref=tot_in.at[h],
            send_sem=tot_send.at[0],
            recv_sem=tot_recv.at[h],
            device_id={"chan": me},
            device_id_type=MESH,
        ).wait_recv()

    if n == heads:
        for k in range(1, n):
            total_arrives(lax.rem(me + k, n))
    else:
        for h in range(heads):
            pl.when(me != h)(functools.partial(total_arrives, h))

    top = tot_in[:, 0, :]
    inverse = tot_in[:, 1, :]
    mean = tot_in[:, 2, :]

    zeros = jnp.zeros((heads, width), BF16)
    spread3 = jnp.concatenate([spread, spread, zeros], axis=0)
    query3 = jnp.concatenate([zeros, zeros, kq_t], axis=0)
    cot_f = cot_rows.astype(F32)
    mixes = []
    for c in range(chans):
        soft = jnp.exp(scores[c] - top) * inverse
        score_grad = soft * (prob[c] - mean)
        high = soft.astype(BF16).astype(F32)
        mix = jnp.concatenate([high, soft - high, score_grad], axis=0).T.astype(BF16)
        mixes.append(mix)
        grad = (dot(mix, spread3) * cot_f).astype(BF16)
        vgrad[pl.ds(c * toks, toks), :] = grad
        img_out[pl.ds(c, 1), :width] = jnp.sum(grad.astype(F32), axis=0, keepdims=True)
        bias_sum = jnp.sum(score_grad, axis=1, keepdims=True)
        img_out[pl.ds(c, 1), width:] = jnp.sum(jnp.where(eye, bias_sum, 0.0), axis=0, keepdims=True)

    img_copies = []
    for k in range(1, g):
        copy = pltpu.make_async_remote_copy(
            src_ref=img_out,
            dst_ref=img_in.at[k - 1],
            send_sem=img_send.at[k],
            recv_sem=img_recv.at[k],
            device_id={"img": lax.rem(my_img + k, g)},
            device_id_type=MESH,
        )
        copy.start()
        img_copies.append(copy)

    stores = []
    for j in range(tiles):
        cols = pl.ds(j * tile, tile)
        acc = dot_t(vgrad[...], pv[cols, :])
        mine = jnp.concatenate([dot(mix, query3[:, j * tile:(j + 1) * tile]) for mix in mixes], axis=0)
        outv[:, cols] = (acc + mine).astype(BF16)
        for c in range(chans):
            copy = pltpu.make_async_copy(
                outv.at[pl.ds(c * toks, toks), cols],
                out_grad.at[c, :, cols],
                store_sem.at[j * chans + c],
            )
            copy.start()
            stores.append(copy)

    sums = img_out[...]
    for k in range(1, g):
        img_copies[k - 1].wait_recv()
        sums = sums + img_in[k - 1]
    high = sums.astype(BF16)
    low = (sums - high.astype(F32)).astype(BF16)
    both = jnp.concatenate([high, low], axis=0)
    parts = dot_t(both[:, :width], pv[...]) + dot(both[:, width:width + heads], kq_t)
    oemb[...] = parts[:chans] + parts[chans:]
    obias[...] = sums[:, width:width + heads]
    for slot, (src, dst) in enumerate(((oemb, out_embed), (obias, out_bias))):
        copy = pltpu.make_async_copy(src, dst, store_sem.at[tiles * chans + slot])
        copy.start()
        stores.append(copy)

    for copy in sends:
        copy.wait_send()
    for k in range(1, n):
        pl.when(lax.rem(me + k, n) < heads)(stat_sends[k - 1].wait_send)
    for copy in img_copies:
        copy.wait_send()
    for copy in stores:
        copy.wait()


def body(n, g, tokens, embed, proj, query, bias, cot):
    chans, toks, width = tokens.shape
    heads = query.shape[1]
    rows = cot.shape[0]
    gather = rows % 16 == 0 and n > 1
    if not gather:
        cot = lax.all_gather(cot, "chan", axis=0, tiled=True)
    tiles = width // min(256, width)
    any_spec = pl.BlockSpec(memory_space=pl.ANY)
    dma = pltpu.SemaphoreType.DMA
    return pl.pallas_call(
        functools.partial(kernel, n, g, gather),
        out_shape=(
            jax.ShapeDtypeStruct((chans, toks, width), BF16),
            jax.ShapeDtypeStruct((chans, width), F32),
            jax.ShapeDtypeStruct((chans, heads), F32),
        ),
        in_specs=[any_spec] * 6,
        out_specs=(any_spec,) * 3,
        scratch_shapes=[
            pltpu.VMEM((chans * toks, width), BF16),
            pltpu.VMEM((chans, width), F32),
            pltpu.VMEM((width, width), BF16),
            pltpu.VMEM((width, heads), BF16),
            pltpu.VMEM(bias.shape, F32),
            pltpu.VMEM((toks, width), BF16),
            pltpu.VMEM((chans * toks, width), BF16),
            pltpu.VMEM((chans * toks, width), BF16),
            pltpu.VMEM((chans * toks, width), BF16),
            pltpu.VMEM((chans * toks, width), BF16),
            pltpu.VMEM((chans, width), F32),
            pltpu.VMEM((chans, heads), F32),
            pltpu.VMEM((heads, 3, toks), F32),
            pltpu.VMEM((n, 3, toks), F32),
            pltpu.VMEM((3, toks), F32),
            pltpu.VMEM((heads, 3, toks), F32),
            pltpu.VMEM((chans, width + 128), F32),
            pltpu.VMEM((max(1, g - 1), chans, width + 128), F32),
            dma((4 + chans + tiles,)),
            dma((tiles * chans + 2,)),
            dma((n,)),
            dma((n,)),
            dma((n,)),
            dma((n,)),
            dma((n,)),
            dma((n,)),
            dma((g,)),
            dma((g,)),
        ],
        compiler_params=pltpu.CompilerParams(
            collective_id=0, has_side_effects=True, vmem_limit_bytes=40 * 1024 * 1024
        ),
    )(tokens, embed, proj, query, bias, cot)


def solution(mesh):
    in_specs = (P("chan", "img", None), P("chan", None), P(), P(), P(), P(("img", "chan"), None))
    out_specs = (P("chan", "img", None), P("chan", None), P("chan", None))
    call = functools.partial(body, mesh.shape["chan"], mesh.shape["img"])
    return jax.shard_map(call, mesh=mesh, in_specs=in_specs, out_specs=out_specs, check_vma=False)
```

time: 141 us -> 39.4 us (0.28)
  blocking collectives: 86 us -> 0 us
  local copies, waits for them, and re-layouts: 42.7 us -> 8.1 us
  Pallas kernels: 0 us -> 30.2 us
  other arithmetic: 5.67 us -> 0 us
  matrix products: 4.38 us -> 0 us
    all_gather x4 -> x0, blocking collectives: 80.3 us -> none  [the longest x3 55.8 us: merged(): pieces = jax.tree.map(lambda part: lax.all_gather(part, axis), value)]
    pallas_call x0 -> x1, Pallas kernels: none -> 30.2 us  [body(): pl.pallas_call(functools.partial(kernel, n, g, gather), out_shape=(jax.Sh...]
    dynamic_slice x32 -> x0, local copies, waits for them, and re-layouts: 29.8 us -> none  [the longest x30 28.8 us: merged(): lax.scan(lambda running, slab: (join(running, slab), None), head, tail)]
    slice x9 -> x0, local copies, waits for them, and re-layouts: 8.07 us -> none  [the longest x6 7.35 us: merged(): tail = jax.tree.map(lambda part: part[1:], pieces)]
    unnamed x15 -> x13, local copies, waits for them, and re-layouts: 1.11 us -> 8.1 us
    psum x1 -> x0, blocking collectives: 5.65 us -> none  [body(): grad_embed, grad_bias = lax.psum((embed_part, bias_part), 'img')]
    dot_general x4 -> x0, matrix products: 4.38 us -> none  [the longest x1 2.25 us: head_parts(): jnp.dot(flat_rows, value_proj, preferred_element_type=jnp.float32)]
    convert_element_type x2 -> x0, other arithmetic: 2.4 us -> none  [the longest x1 1.45 us: body(): (tokens.astype(jnp.float32) + chan_embed[:, None, :]).astype(jnp.bfloat16)]
where the time goes in v1:
time: 39.4 us; the launch traced here: 39 us
  Pallas kernels  30.2 us (77%)
  local copies, waits for them, and re-layouts  8.1 us (21%)
  between operations  0.66 us (2%)
    pallas_call x1, Pallas kernels, body(): pl.pallas_call(functools.partial(kernel, n, g, gather), out_shape=(jax.Sh...  30.2 us
    unnamed x13, local copies, waits for them, and re-layouts  8.1 us

profile of v1, /device:TPU:0, one launch (start us, length us, event | category | flops | bytes accessed | tf_op | source)
XLA Modules:
  0.0 39.0 jit_solution(16253534618349183208)
XLA Ops:
  0.6 0.8 %copy.10.bias = f32[32,16]{1,0:T(8,128)S(1)} copy(f32[32,16]{0,1:T(8,128)} %param.10) | data formatting | bytes 4096 | tf_op args[4]
  1.4 0.9 %copy.9.query = bf16[1024,16]{1,0:T(8,128)(2,1)S(1)} copy(bf16[1024,16]{0,1:T(8,128)(2,1)} %param.9) | data formatting | bytes 65536 | tf_op args[3]
  2.3 0.0 copy-start
  2.3 1.6 %copy-done = bf16[1024,1024]{1,0:T(8,128)(2,1)S(1)} copy-done((bf16[1024,1024]{1,0:T(8,128)(2,1)S(1)}, bf16[1024,1024]{1,0:T(8,128)(2,1)}, u32[]{:S(2)}) %copy-start) | copy-done | bytes 2097176
  3.9 0.0 copy-start.1
  3.9 1.2 %copy-done.1 = bf16[2,256,1024]{2,1,0:T(8,128)(2,1)S(1)} copy-done((bf16[2,256,1024]{2,1,0:T(8,128)(2,1)S(1)}, bf16[2,256,1024]{2,1,0:T(8,128)(2,1)}, u32[]{:S(2)}) %copy-start.1) | copy-done | bytes 1048600
  5.2 0.0 copy-start.2
  5.2 0.8 %copy-done.2 = bf16[16,1024]{1,0:T(8,128)(2,1)S(1)} copy-done((bf16[16,1024]{1,0:T(8,128)(2,1)S(1)}, bf16[16,1024]{1,0:T(8,128)(2,1)}, u32[]{:S(2)}) %copy-start.2) | copy-done | bytes 32792
  5.9 0.0 copy-start.3
  5.9 0.7 %copy-done.3 = f32[2,1024]{1,0:T(2,128)S(1)} copy-done((f32[2,1024]{1,0:T(2,128)S(1)}, f32[2,1024]{1,0:T(2,128)}, u32[]{:S(2)}) %copy-start.3) | copy-done | bytes 8216
  6.6 30.2 %shard_map.85 = (bf16[2,256,1024]{2,1,0:T(8,128)(2,1)S(1)}, f32[2,1024]{1,0:T(2,128)S(1)}, f32[2,16]{1,0:T(2,128)S(1)}) custom-call(bf16[2,256,1024]{2,1,0:T(8,128)(2,1)S(1)} %copy-done.1, f32[2,1024]{1,0:T(2,128)S(1)} %copy-done.3, bf16[1024,1024]{1,0:T(8,128)(2,1)S(1)} %copy-done, bf16[1024,16]{1,0:T(8,128)(2,1)S(1)} %copy.9.query, ...), custom_call_target="tpu_custom_call" | custom-call | tf_op jit(solution)/shard_map/pallas_call | solution.py:370
  36.8 1.0 %copy.14 = bf16[2,256,1024]{2,1,0:T(8,128)(2,1)} copy(bf16[2,256,1024]{2,1,0:T(8,128)(2,1)S(1)} %get-tuple-element.6) | data formatting | bytes 2097152
  37.8 0.6 %copy.15 = f32[2,1024]{1,0:T(2,128)} copy(f32[2,1024]{1,0:T(2,128)S(1)} %get-tuple-element.7) | data formatting | bytes 16384
  38.4 0.6 %copy.16 = f32[2,16]{1,0:T(2,128)} copy(f32[2,16]{1,0:T(2,128)S(1)} %get-tuple-element.8) | data formatting | bytes 256
Async XLA Ops:
  2.3 1.6 %copy-start = (bf16[1024,1024]{1,0:T(8,128)(2,1)S(1)}, bf16[1024,1024]{1,0:T(8,128)(2,1)}, u32[]{:S(2)}) copy-start(bf16[1024,1024]{1,0:T(8,128)(2,1)} %proj.1) | copy-start | bytes 6291460
  3.9 1.2 %copy-start.1 = (bf16[2,256,1024]{2,1,0:T(8,128)(2,1)S(1)}, bf16[2,256,1024]{2,1,0:T(8,128)(2,1)}, u32[]{:S(2)}) copy-start(bf16[2,256,1024]{2,1,0:T(8,128)(2,1)} %tokens.1) | copy-start | bytes 3145732
  5.2 0.8 %copy-start.2 = (bf16[16,1024]{1,0:T(8,128)(2,1)S(1)}, bf16[16,1024]{1,0:T(8,128)(2,1)}, u32[]{:S(2)}) copy-start(bf16[16,1024]{1,0:T(8,128)(2,1)} %cot.1) | copy-start | bytes 98308
  5.9 0.7 %copy-start.3 = (f32[2,1024]{1,0:T(2,128)S(1)}, f32[2,1024]{1,0:T(2,128)}, u32[]{:S(2)}) copy-start(f32[2,1024]{1,0:T(2,128)} %embed.1) | copy-start | bytes 24580

commit v2 on v1

v2 whole, which is shorter than its diff:
```python
import functools

import jax
import jax.numpy as jnp
from jax import lax
from jax.experimental import pallas as pl
from jax.experimental.pallas import tpu as pltpu
from jax.sharding import PartitionSpec as P

MESH = pl.DeviceIdType.MESH
F32 = jnp.float32
BF16 = jnp.bfloat16
ROWS_BY_ROWS = (((1,), (1,)), ((), ()))


def dot_t(left, right):
    return lax.dot_general(left, right, ROWS_BY_ROWS, preferred_element_type=F32)


def dot(left, right):
    return jnp.dot(left, right, preferred_element_type=F32)


def grid_of(n):
    chips = n // 2
    wide = 1
    while wide * wide * 4 <= chips:
        wide *= 2
    return chips // wide, wide


def far_first(n):
    return sorted(range(1, n), key=lambda k: -min(k, n - k))


def kernel(
    n, g, gather,
    tokens, embed, proj, query, bias, cot,
    out_grad, out_embed, out_bias,
    tok, emb, pv, kq, bia, cots, shifted, values, vgrad, acc, outv, oemb, obias,
    stat_out, stat_in, tot_out, tot_in, mean_out, mean_in, avg_out, avg_in,
    img_out, img_in, gb_out, gb_in,
    load_sem, store_sem, cot_send, cot_recv, stat_send, stat_recv, tot_send, tot_recv,
    mean_send, mean_recv, avg_send, avg_recv, img_send, img_recv, gb_send, gb_recv,
):
    chans, toks, width = tokens.shape
    heads = query.shape[0]
    depth = width // heads
    tile = min(256, width)
    tiles = width // tile
    me = lax.axis_index("chan")
    my_img = lax.axis_index("img")
    rows = cot.shape[0]

    def load(slot, src, dst):
        copy = pltpu.make_async_copy(src, dst, load_sem.at[slot])
        copy.start()
        return copy

    if gather:
        cot_load = load(0, cot, cots.at[pl.ds(pl.multiple_of(me * rows, rows), rows)])
    else:
        cot_load = load(0, cot, cots)
    small_loads = [load(1, embed, emb), load(2, bias, bia), load(3, query, kq)]
    tok_loads = [load(4 + c, tokens.at[c], tok.at[pl.ds(c * toks, toks)]) for c in range(chans)]
    proj_loads = [
        load(
            4 + chans + j,
            proj.at[:, pl.ds(j * tile, tile)],
            pv.at[:, pl.ds(j * tile, tile)],
        )
        for j in range(tiles)
    ]

    barrier = pltpu.get_barrier_semaphore()
    for k in far_first(n):
        pl.semaphore_signal(
            barrier, inc=1, device_id={"chan": lax.rem(me + k, n)}, device_id_type=MESH
        )
    for k in range(1, g):
        pl.semaphore_signal(
            barrier, inc=1, device_id={"img": lax.rem(my_img + k, g)}, device_id_type=MESH
        )

    tall, wide = grid_of(n)
    core = lax.rem(me, 2)
    my_b = lax.rem(me // 2, wide)
    my_a = me // (2 * wide)

    def index(a, b, c):
        return (a * wide + b) * 2 + c

    sends = []

    def block(i):
        return cots.at[pl.ds(pl.multiple_of(i * rows, rows), rows)]

    def send(i, to, own=False):
        copy = pltpu.make_async_remote_copy(
            src_ref=cot if own else block(i),
            dst_ref=block(i),
            send_sem=cot_send.at[len(sends)],
            recv_sem=cot_recv.at[i],
            device_id={"chan": to},
            device_id_type=MESH,
        )
        copy.start()
        sends.append(copy)

    def arrive(i):
        pltpu.make_async_remote_copy(
            src_ref=cot,
            dst_ref=block(i),
            send_sem=cot_send.at[0],
            recv_sem=cot_recv.at[i],
            device_id={"chan": me},
            device_id_type=MESH,
        ).wait_recv()

    def others_a():
        return [lax.rem(my_a + k, tall) for k in far_first(tall)]

    def others_b():
        return [lax.rem(my_b + k, wide) for k in range(1, wide)]

    pl.semaphore_wait(barrier, n - 1 + g - 1)
    mate = index(my_a, my_b, 1 - core)
    if gather:
        for a in others_a():
            send(me, index(a, my_b, core), own=True)
        for b in others_b():
            send(me, index(my_a, b, core), own=True)
        send(me, mate, own=True)

    for copy in small_loads:
        copy.wait()
    kq_t = kq[...]
    head_at = lax.broadcasted_iota(jnp.int32, (heads, width), 0) * depth
    lane_at = lax.broadcasted_iota(jnp.int32, (heads, width), 1)
    spread_f = jnp.where((lane_at >= head_at) & (lane_at < head_at + depth), 1.0, 0.0)
    spread = spread_f.astype(BF16)
    eye = lax.broadcasted_iota(jnp.int32, (heads, 128), 0) == lax.broadcasted_iota(
        jnp.int32, (heads, 128), 1
    )
    bias_all = bia[...]
    bias_at = lax.broadcasted_iota(jnp.int32, bias_all.shape, 1)

    scores = []
    for c in range(chans):
        tok_loads[c].wait()
        at = pl.ds(c * toks, toks)
        moved = (tok[at, :].astype(F32) + emb[pl.ds(c, 1), :]).astype(BF16)
        shifted[at, :] = moved
        mine = bias_at == me * chans + c
        bias_col = jnp.sum(jnp.where(mine, bias_all, 0.0), axis=1, keepdims=True)
        scores.append(dot_t(kq_t, moved) + bias_col)

    peak = functools.reduce(jnp.maximum, scores)
    stat_out[:, 0, :] = peak
    exps = [jnp.exp(s - peak) for s in scores]
    stat_out[:, 1, :] = functools.reduce(jnp.add, exps)

    def to_owners(src, dst, send_sem, recv_sem):
        copies = []
        for k in far_first(n):
            to = lax.rem(me + k, n)
            copy = pltpu.make_async_remote_copy(
                src_ref=src.at[lax.rem(to, heads)],
                dst_ref=dst.at[me],
                send_sem=send_sem.at[k],
                recv_sem=recv_sem.at[me],
                device_id={"chan": to},
                device_id_type=MESH,
            )
            pl.when(to < heads)(copy.start) if n > heads else copy.start()
            copies.append(copy)
        return copies

    def to_all(src, dst, send_sem, recv_sem):
        slot = lax.rem(me, heads)
        copies = []
        for k in far_first(n):
            copy = pltpu.make_async_remote_copy(
                src_ref=src,
                dst_ref=dst.at[slot],
                send_sem=send_sem.at[k],
                recv_sem=recv_sem.at[slot],
                device_id={"chan": lax.rem(me + k, n)},
                device_id_type=MESH,
            )
            copy.start()
            copies.append(copy)
        dst[slot] = src[...]
        return copies

    def landed(dst, recv_sem, slot):
        pltpu.make_async_remote_copy(
            src_ref=dst.at[slot],
            dst_ref=dst.at[slot],
            send_sem=load_sem.at[0],
            recv_sem=recv_sem.at[slot],
            device_id={"chan": me},
            device_id_type=MESH,
        ).wait_recv()

    def if_owner(work):
        if n == heads:
            work()
        else:
            pl.when(me < heads)(work)

    def all_landed(dst, recv_sem):
        if n == heads:
            for k in range(1, n):
                landed(dst, recv_sem, lax.rem(me + k, n))
        else:
            for h in range(heads):
                pl.when(me != h)(functools.partial(landed, dst, recv_sem, h))

    owner_sends = [(stat_out, stat_in, stat_send, stat_recv), (mean_out, mean_in, mean_send, mean_recv)]
    sent = [to_owners(*owner_sends[0])]

    def combine_totals():
        stat_in[me] = stat_out[lax.rem(me, heads)]
        for k in range(1, n):
            landed(stat_in, stat_recv, lax.rem(me + k, n))
        peaks = stat_in[:, 0, :]
        top = jnp.max(peaks, axis=0, keepdims=True)
        total = jnp.sum(stat_in[:, 1, :] * jnp.exp(peaks - top), axis=0, keepdims=True)
        tot_out[0:1, :] = top
        tot_out[1:2, :] = 1.0 / total
        for copy in to_all(tot_out, tot_in, tot_send, tot_recv):
            copy.wait_send()

    def combine_means():
        mean_in[me] = mean_out[lax.rem(me, heads)]
        for k in range(1, n):
            landed(mean_in, mean_recv, lax.rem(me + k, n))
        scale = jnp.exp(stat_in[:, 0, :] - tot_out[0:1, :])
        avg_out[...] = jnp.sum(mean_in[:, 0, :] * scale, axis=0, keepdims=True) * tot_out[1:2, :]
        for copy in to_all(avg_out, avg_in, avg_send, avg_recv):
            copy.wait_send()

    def value_tile(j):
        proj_loads[j].wait()
        cols = pl.ds(j * tile, tile)
        values[:, cols] = dot(shifted[...], pv[:, cols]).astype(BF16)

    for j in range(tiles):
        value_tile(j)
    if gather:
        for a in others_a():
            i = index(a, my_b, core)
            arrive(i)
            for b in others_b():
                send(i, index(my_a, b, core))
            send(i, mate)
    if_owner(combine_totals)
    if gather:
        for b in others_b():
            for k in range(tall):
                i = index(lax.rem(my_a + k, tall), b, core)
                arrive(i)
                send(i, mate)
    cot_load.wait()
    if gather:
        for a in range(tall):
            for b in range(wide):
                arrive(index(a, b, 1 - core))

    prob = [dot_t(spread, values[pl.ds(c * toks, toks), :] * cots[...]) for c in range(chans)]
    mean_out[:, 0, :] = functools.reduce(jnp.add, [e * p for e, p in zip(exps, prob)])
    sent.append(to_owners(*owner_sends[1]))

    all_landed(tot_in, tot_recv)
    soft = [jnp.exp(s - tot_in[:, 0, :]) * tot_in[:, 1, :] for s in scores]
    spread2 = jnp.concatenate([spread, spread], axis=0)
    for c in range(chans):
        high = soft[c].astype(BF16).astype(F32)
        mix = jnp.concatenate([high, soft[c] - high], axis=0).T.astype(BF16)
        grad = (dot(mix, spread2) * cots[...].astype(F32)).astype(BF16)
        vgrad[pl.ds(c * toks, toks), :] = grad
        img_out[pl.ds(c, 1), :] = jnp.sum(grad.astype(F32), axis=0, keepdims=True)

    def to_images(src, dst, send_sem, recv_sem):
        copies = []
        for k in range(1, g):
            copy = pltpu.make_async_remote_copy(
                src_ref=src,
                dst_ref=dst.at[k - 1],
                send_sem=send_sem.at[k],
                recv_sem=recv_sem.at[k],
                device_id={"img": lax.rem(my_img + k, g)},
                device_id_type=MESH,
            )
            copy.start()
            copies.append(copy)
        return copies

    def total_of(copies, src, dst):
        sums = src[...]
        for k, copy in enumerate(copies):
            copy.wait_recv()
            sums = sums + dst[k]
        return sums

    img_copies = to_images(img_out, img_in, img_send, img_recv)
    for j in range(tiles):
        cols = pl.ds(j * tile, tile)
        acc[:, cols] = dot_t(vgrad[...], pv[cols, :])

    if_owner(combine_means)

    def halves(sums):
        high = sums.astype(BF16)
        return jnp.concatenate([high, (sums - high.astype(F32)).astype(BF16)], axis=0)

    embed_part = dot_t(halves(total_of(img_copies, img_out, img_in)), pv[...])

    all_landed(avg_in, avg_recv)
    mean = avg_in[:, 0, :]
    slopes = []
    for c in range(chans):
        score_grad = soft[c] * (prob[c] - mean)
        slopes.append(score_grad)
        bias_sum = jnp.sum(score_grad, axis=1, keepdims=True)
        gb_out[pl.ds(c, 1), :] = jnp.sum(jnp.where(eye, bias_sum, 0.0), axis=0, keepdims=True)
    gb_copies = to_images(gb_out, gb_in, gb_send, gb_recv)

    stores = []

    def store(src, dst):
        copy = pltpu.make_async_copy(src, dst, store_sem.at[len(stores)])
        copy.start()
        stores.append(copy)

    for c in range(chans):
        at = pl.ds(c * toks, toks)
        outv[c] = (acc[at, :] + dot(slopes[c].T.astype(BF16), kq_t)).astype(BF16)
        store(outv.at[c], out_grad.at[c])

    bias_total = total_of(gb_copies, gb_out, gb_in)[:, :heads]
    parts = embed_part + dot(halves(bias_total), kq_t)
    oemb[...] = parts[:chans] + parts[chans:]
    obias[...] = bias_total
    store(oemb, out_embed)
    store(obias, out_bias)

    for copy in sends + img_copies + gb_copies:
        copy.wait_send()
    for copies in sent:
        for k, copy in zip(far_first(n), copies):
            pl.when(lax.rem(me + k, n) < heads)(copy.wait_send) if n > heads else copy.wait_send()
    for copy in stores:
        copy.wait()


def leave(*refs):
    count = len(refs) // 2
    sems = refs[-1]
    copies = [
        pltpu.make_async_copy(refs[i], refs[count + i], sems.at[i]) for i in range(count)
    ]
    for copy in copies:
        copy.start()
    for copy in copies:
        copy.wait()


def body(n, g, tokens, embed, proj, query, bias, cot):
    chans, toks, width = tokens.shape
    heads = query.shape[1]
    rows = cot.shape[0]
    gather = rows % 16 == 0 and n > 1
    if not gather:
        cot = lax.all_gather(cot, "chan", axis=0, tiled=True)
    tiles = width // min(256, width)
    any_spec = pl.BlockSpec(memory_space=pl.ANY)
    hbm_spec = pl.BlockSpec(memory_space=pltpu.HBM)
    dma = pltpu.SemaphoreType.DMA
    shapes = (
        jax.ShapeDtypeStruct((chans, toks, width), BF16),
        jax.ShapeDtypeStruct((chans, width), F32),
        jax.ShapeDtypeStruct((chans, heads), F32),
    )
    results = pl.pallas_call(
        functools.partial(kernel, n, g, gather),
        out_shape=tuple(pltpu.VMEM(x.shape, x.dtype) for x in shapes),
        in_specs=[hbm_spec] * 6,
        out_specs=(pl.BlockSpec(memory_space=pltpu.VMEM),) * 3,
        scratch_shapes=[
            pltpu.VMEM((chans * toks, width), BF16),
            pltpu.VMEM((chans, width), F32),
            pltpu.VMEM((width, width), BF16),
            pltpu.VMEM((heads, width), BF16),
            pltpu.VMEM(bias.shape[::-1], F32),
            pltpu.VMEM((toks, width), BF16),
            pltpu.VMEM((chans * toks, width), BF16),
            pltpu.VMEM((chans * toks, width), BF16),
            pltpu.VMEM((chans * toks, width), BF16),
            pltpu.VMEM((chans * toks, width), F32),
            pltpu.VMEM((chans, toks, width), BF16),
            pltpu.VMEM((chans, width), F32),
            pltpu.VMEM((chans, heads), F32),
            pltpu.VMEM((heads, 2, toks), F32),
            pltpu.VMEM((n, 2, toks), F32),
            pltpu.VMEM((2, toks), F32),
            pltpu.VMEM((heads, 2, toks), F32),
            pltpu.VMEM((heads, 1, toks), F32),
            pltpu.VMEM((n, 1, toks), F32),
            pltpu.VMEM((1, toks), F32),
            pltpu.VMEM((heads, 1, toks), F32),
            pltpu.VMEM((chans, width), F32),
            pltpu.VMEM((max(1, g - 1), chans, width), F32),
            pltpu.VMEM((chans, 128), F32),
            pltpu.VMEM((max(1, g - 1), chans, 128), F32),
            dma((4 + chans + tiles,)),
            dma((chans + 2,)),
        ]
        + [dma((n,))] * 10
        + [dma((g,))] * 4,
        compiler_params=pltpu.CompilerParams(
            collective_id=0, has_side_effects=True, vmem_limit_bytes=60 * 1024 * 1024
        ),
    )(tokens, embed, proj, query.T, bias.T, cot)
    return pl.pallas_call(
        leave,
        out_shape=shapes,
        in_specs=[any_spec] * 3,
        out_specs=(hbm_spec,) * 3,
        scratch_shapes=[dma((3,))],
        compiler_params=pltpu.CompilerParams(vmem_limit_bytes=4 * 1024 * 1024),
    )(*results)


def solution(mesh):
    in_specs = (P("chan", "img", None), P("chan", None), P(), P(), P(), P(("img", "chan"), None))
    out_specs = (P("chan", "img", None), P("chan", None), P("chan", None))
    call = functools.partial(body, mesh.shape["chan"], mesh.shape["img"])
    return jax.shard_map(call, mesh=mesh, in_specs=in_specs, out_specs=out_specs, check_vma=False)
```

time: 39.4 us -> 30.1 us (0.76)
  local copies, waits for them, and re-layouts: 8.1 us -> 0 us
  Pallas kernels: 30.2 us -> 29.3 us
    unnamed x13 -> x0, local copies, waits for them, and re-layouts: 8.1 us -> none
    pallas_call x1 -> x2, Pallas kernels: 30.2 us -> 29.3 us  [the longest x1 28.3 us: body(): pl.pallas_call(functools.partial(kernel, n, g, gather), out_shape=tuple((...]
where the time goes in v2:
time: 30.1 us; the launch traced here: 30 us
  Pallas kernels  29.3 us (97%)
  between operations  0.64 us (2%)
    pallas_call x1, Pallas kernels, body(): pl.pallas_call(functools.partial(kernel, n, g, gather), out_shape=tuple((...  28.3 us
    pallas_call x1, Pallas kernels, body(): pl.pallas_call(leave, out_shape=shapes, in_specs=[any_spec] * 3, out_spec...  1 us

profile of v2, /device:TPU:0, one launch (start us, length us, event | category | flops | bytes accessed | tf_op | source)
XLA Modules:
  0.0 30.0 jit_solution(2131271156219033062)
XLA Ops:
  0.6 28.3 %shard_map.85 = (bf16[2,256,1024]{2,1,0:T(8,128)(2,1)S(1)}, f32[2,1024]{1,0:T(2,128)S(1)}, f32[2,16]{1,0:T(2,128)S(1)}) custom-call(bf16[2,256,1024]{2,1,0:T(8,128)(2,1)} %tokens.1, f32[2,1024]{1,0:T(2,128)} %embed.1, bf16[1024,1024]{1,0:T(8,128)(2,1)} %proj.1, bf16[16,1024]{1,0:T(8,128)(2,1)} %bitcast.2, f32[16,32]{1,0:T(8,128)} %bitcast.3, ...), custom_call_target="tpu_custom_call" | custom-call | tf_op jit(solution)/shard_map/pallas_call | solution.py:386
  29.0 1.0 %shard_map.86 = (bf16[2,256,1024]{2,1,0:T(8,128)(2,1)}, f32[2,1024]{1,0:T(2,128)}, f32[2,16]{1,0:T(2,128)}) custom-call(bf16[2,256,1024]{2,1,0:T(8,128)(2,1)S(1)} %get-tuple-element.6.refs_0_, f32[2,1024]{1,0:T(2,128)S(1)} %get-tuple-element.7.refs_1_, f32[2,16]{1,0:T(2,128)S(1)} %get-tuple-element.8.refs_2_), custom_call_target="tpu_custom_call" | custom-call | tf_op jit(solution)/shard_map/pallas_call | solution.py:426
